TPU v7x, 128 devices: a whole 4x4x4 slice. The times are simulated.
128 devices in a mesh: section: 4 (over x_hi, core), shard: 32 (over x_lo, z, y).
Axes of the slice: x: 4 (x_hi: 2, x_lo: 2; x = x_hi * 2 + x_lo), y: 4, z: 4, core: 2. Of those that a mesh axis runs over, the one named last changes fastest.
Arguments:
- hidden: bfloat16 [1024, 8192], P(('section', 'shard')), may hold values from -6 to 6
- norm_gain: float32 [4, 8192], P('section'), may hold values from 0.1 to 1.9
- gate_weight: bfloat16 [4, 8192, 16384], P('section', None, 'shard'), may hold values from -0.0625 to 0.0625
- up_weight: bfloat16 [4, 8192, 16384], P('section', None, 'shard'), may hold values from -0.0625 to 0.0625
- head_vector: bfloat16 [4, 16384], P('section', 'shard'), may hold values from -0.046875 to 0.046875
- pack_slot: int32 [4, 1024], replicated, may hold values from 0 to 1023, each once within a row
- owner_slot: int32 [1024], replicated, may hold values from 0 to 1023, each once
Outputs:
- section_scores: float32 [4, 1024], P('section', 'shard')
- joined: float32 [4, 1024], P(None, ('section', 'shard'))
All inputs are finite; a program needn't handle non-finite values.
Results may differ from a plain program's by a relative error of at most 0.0032.
Values may be sent and summed in bfloat16 or wider, within the bound.
No kernel may reach another device: no remote copies, remote signals or barrier semaphores. Data moves between devices by JAX's collectives and lax.ppermute only.
A program may use at most 128 MiB of HBM per device.

v0:
```python
import jax
import jax.numpy as jnp
from jax import lax
from jax.sharding import PartitionSpec as P

epsilon = 1e-06


def normalize(row_block, gain_row):
    widened = row_block.astype(jnp.float32)
    inv_rms = lax.rsqrt(jnp.mean(widened * widened, axis=1, keepdims=True) + epsilon)
    return (widened * inv_rms * gain_row).astype(jnp.bfloat16)


def score_block(normed, gate_cols, up_cols, head_cols):
    gate_out = jnp.dot(normed, gate_cols, preferred_element_type=jnp.float32)
    up_out = jnp.dot(normed, up_cols, preferred_element_type=jnp.float32)
    activated = jax.nn.silu(gate_out) * up_out
    return jnp.dot(activated, head_cols.astype(jnp.float32), precision=lax.Precision.HIGHEST)


def invert(ordering):
    total_rows = ordering.shape[0]
    return (
        jnp.zeros((total_rows,), jnp.int32)
        .at[ordering]
        .set(jnp.arange(total_rows, dtype=jnp.int32))
    )


def body(hidden, norm_gain, gate_weight, up_weight, head_vector, pack_slot, owner_slot):
    gain_row = norm_gain[0]
    gate_cols = gate_weight[0]
    up_cols = up_weight[0]
    head_cols = head_vector[0]
    partial_value = score_block(
        normalize(lax.all_gather(hidden, ("section", "shard"), axis=0, tiled=True), gain_row),
        gate_cols,
        up_cols,
        head_cols,
    )
    section = lax.axis_index("section")
    own_pack = lax.dynamic_index_in_dim(pack_slot, section, 0, keepdims=False)
    inverse = invert(own_pack)
    packed = partial_value[inverse]
    scores = lax.psum_scatter(packed, "shard", scatter_dimension=0, tiled=True)
    flipped = jnp.logical_or(section == 1, section == 3)
    values = jnp.where(flipped, jax.nn.log_sigmoid(scores), scores)
    shards = lax.axis_size("shard")
    sections = lax.axis_size("section")
    pack_rows = values.shape[0]
    total_rows = owner_slot.shape[0]
    own_count = total_rows // (shards * sections)
    first_row = lax.axis_index("shard") * pack_rows
    rows_here = lax.dynamic_slice_in_dim(inverse, first_row, pack_rows)
    targets = owner_slot[rows_here]
    spread = jnp.zeros((total_rows,), jnp.float32).at[targets].set(values)
    spread = spread.reshape(sections * shards, own_count)
    arrived = lax.all_to_all(spread, ("section", "shard"), split_axis=0, concat_axis=0, tiled=True)
    joined = arrived.reshape(sections, shards, own_count).sum(axis=1)
    return (values[None, :], joined)


def solution(mesh):
    in_specs = (
        P(("section", "shard"), None),
        P("section", None),
        P("section", None, "shard"),
        P("section", None, "shard"),
        P("section", "shard"),
        P(),
        P(),
    )
    out_specs = (P("section", "shard"), P(None, ("section", "shard")))
    return jax.shard_map(body, mesh=mesh, in_specs=in_specs, out_specs=out_specs, check_vma=False)
```

profile of v0, /device:TPU:1, one launch (start us, length us, event | category | flops | bytes accessed | tf_op | source)
XLA Modules:
  0.0 487.9 jit_solution(15857791865865555446)
XLA Ops:
  7.2 0.0 copy-start
  7.2 0.0 all-gather.2.cloned.1.call-start
  7.2 0.7 all-gather.2.cloned.1.call-update
  7.9 0.7 compare_select_fusion
  8.7 4.3 scatter_custom_fusion
  13.0 1.2 dynamic-slice
  14.9 0.1 compare_select_fusion.3
  15.0 0.0 copy-start.2
  15.0 0.7 gather_fusion.1
  15.7 324.4 %all-gather.2.cloned.1.call-done = bf16[1024,8192]{1,0:T(8,128)(2,1)} async-done(((bf16[8,8192]{1,0:T(8,128)(2,1)}), bf16[1024,8192]{1,0:T(8,128)(2,1)}) %all-gather.2.cloned.1.call-update) | async-done | bytes 16777232 | tf_op jit(solution)/shard_map/all_gather | solution.py:37
  340.1 7.5 %fusion = f32[1024]{0:T(1024)S(1)} fusion(bf16[1024,8192]{1,0:T(8,128)(2,1)} %all-gather.2.cloned.1.call-done), kind=kLoop, calls=%fused_computation.6 | loop fusion | flops 25164800 | bytes 16781312 | tf_op jit(solution)/shard_map/reduce_sum | solution.py:11
  347.7 3.1 copy-done.1
  350.8 12.7 %fusion.3 = f32[1024,512]{1,0:T(8,128)} fusion(bf16[1,8192,512]{2,1,0:T(8,128)(2,1)} %param.10, bf16[1024,8192]{1,0:T(8,128)(2,1)S(1)} %copy-done.1, f32[8192]{0:T(1024)S(1)} %bitcast.28, f32[1024]{0:T(1024)S(1)} %add_rsqrt_fusion), kind=kOutput, calls=%fused_computation.9 | convolution fusion | flops 8623489024 | bytes 27299840 | tf_op jit(solution)/shard_map/dot_general | solution.py:17
  363.5 12.7 %fusion.5 = f32[1024,512]{1,0:T(8,128)} fusion(bf16[1,8192,512]{2,1,0:T(8,128)(2,1)} %param.9, bf16[1024,8192]{1,0:T(8,128)(2,1)S(1)} %copy-done.1, f32[8192]{0:T(1024)S(1)} %bitcast.29, f32[1024]{0:T(1024)S(1)} %add_rsqrt_fusion), kind=kOutput, calls=%fused_computation.11 | convolution fusion | flops 8623489024 | bytes 27299840 | tf_op jit(solution)/shard_map/dot_general | solution.py:16
  376.2 3.7 fusion.9
  380.0 4.5 gather_fusion
  384.5 69.1 %all-reduce = f32[1024]{0:T(1024)S(1)} all-reduce(f32[1024]{0:T(1024)S(1)} %gather_fusion), channel_id=2, replica_groups=mesh['section'=4,'shard'=32] {'shard'}, use_global_device_ids=true, to_apply=%region_2.3.clone | all-reduce | flops 1024 | bytes 8192
  453.6 0.1 broadcast_select_fusion
  453.7 0.7 scatter_custom_fusion.1
  454.4 0.7 all_to_all.6
  455.1 15.7 %all-to-all-start = ((f32[128,1,8]{2,1,0:T(1,128)}), f32[128,1,8]{2,1,0:T(1,128)S(1)}, u32[]{:S(2)}, u32[]{:S(2)}) async-start(f32[128,1,8]{2,1,0:T(1,128)} %bitcast.9), calls=%async_computation | async-start | bytes 131072 | tf_op jit(solution)/shard_map/all_to_all | solution.py:59
  470.8 0.6 fusion.26
  471.4 9.0 %all-to-all-done = f32[128,1,8]{2,1,0:T(1,128)S(1)} async-done(((f32[128,1,8]{2,1,0:T(1,128)}), f32[128,1,8]{2,1,0:T(1,128)S(1)}, u32[]{:S(2)}, u32[]{:S(2)}) %all-to-all-start) | async-done | bytes 4128 | tf_op jit(solution)/shard_map/all_to_all | solution.py:59
  480.4 0.6 bitcast_reduce_fusion
  (10 shorter events, 0.0 us)
Async XLA Ops:
  7.2 7.8 %copy-start = (s32[1024]{0:T(1024)S(1)}, s32[1024]{0:T(1024)}, u32[]{:S(2)}) copy-start(s32[1024]{0:T(1024)} %param.13) | copy-start | bytes 12292
  7.2 333.0 %all-gather.2.cloned.1.call-start = ((), (), s32[]{:S(2)}) async-start(), calls=%async_computation.1 | async-start | bytes 16908288 | tf_op jit(solution)/shard_map/all_gather | solution.py:37
  15.0 332.7 %copy-start.2 = (f32[1,8192]{1,0:T(1,128)S(1)}, f32[1,8192]{1,0:T(1,128)}, u32[]{:S(2)}) copy-start(f32[1,8192]{1,0:T(1,128)} %param.8) | copy-start | bytes 98308
  340.1 10.7 %copy-start.1 = (bf16[1024,8192]{1,0:T(8,128)(2,1)S(1)}, bf16[1024,8192]{1,0:T(8,128)(2,1)}, u32[]{:S(2)}) copy-start(bf16[1024,8192]{1,0:T(8,128)(2,1)} %all-gather.2.cloned.1.call-done) | copy-start | bytes 50331652
  363.5 12.7 %copy-start.3 = (bf16[1,512]{1,0:T(2,128)(2,1)S(1)}, bf16[1,512]{1,0:T(2,128)(2,1)}, u32[]{:S(2)}) copy-start(bf16[1,512]{1,0:T(2,128)(2,1)} %param.11) | copy-start | bytes 3076
  455.1 25.3 %all-to-all-start = ((f32[128,1,8]{2,1,0:T(1,128)}), f32[128,1,8]{2,1,0:T(1,128)S(1)}, u32[]{:S(2)}, u32[]{:S(2)}) async-start(f32[128,1,8]{2,1,0:T(1,128)} %bitcast.9), calls=%async_computation | async-start | bytes 131072 | tf_op jit(solution)/shard_map/all_to_all | solution.py:59
Sparse Core Ops, SparseCore 0:
  9.7 330.3 all-gather.1
where the time goes:
time: 488 us
  waiting for transfers between devices  334 us (68%)
  blocking collectives  69.1 us (14%)
  matrix products  29.1 us (6%)
  starting transfers between devices  15.7 us (3%)
  local copies, waits for them, and re-layouts  15.3 us (3%)
  between operations  14.8 us (3%)
  other arithmetic  9.65 us (2%)
    all_gather x1, waiting for transfers between devices, body(): lax.all_gather(hidden, ('section', 'shard'), axis=0, tiled=True)  324 us
    unnamed x1, blocking collectives  69.1 us
    all_to_all x1, starting transfers between devices, body(): lax.all_to_all(spread, ('section', 'shard'), split_axis=0, concat_axis=0,...  15.7 us
    dot_general x1, matrix products, score_block(): up_out = jnp.dot(normed, up_cols, preferred_element_type=jnp.float32)  12.7 us
    dot_general x1, matrix products, score_block(): gate_out = jnp.dot(normed, gate_cols, preferred_element_type=jnp.float32)  12.7 us
  transfers between devices with their start and end apart: 2, of which 2 were waited for; matrix products, arithmetic and copies ran while one was open for 2% of the time, Pallas kernels for 0%

commit v1 on v0

--- a/solution.py
+++ b/solution.py
@@ -34,7 +34,18 @@
     up_cols = up_weight[0]
     head_cols = head_vector[0]
     partial_value = score_block(
-        normalize(lax.all_gather(hidden, ("section", "shard"), axis=0, tiled=True), gain_row),
+        normalize(
+            jnp.concatenate(
+                lax.all_to_all(
+                    jnp.stack([hidden] * lax.axis_size(("section", "shard"))),
+                    ("section", "shard"),
+                    0,
+                    0,
+                ),
+                axis=0,
+            ),
+            gain_row,
+        ),
         gate_cols,
         up_cols,
         head_cols,

time: 488 us -> 385 us (0.79)
  waiting for transfers between devices: 334 us -> 222 us
  starting transfers between devices: 15.7 us -> 34.4 us
  between operations: 14.8 us -> 1.45 us
    all_gather x1 -> x0, waiting for transfers between devices: 324 us -> none  [body(): lax.all_gather(hidden, ('section', 'shard'), axis=0, tiled=True)]
    all_to_all x0 -> x1, waiting for transfers between devices: none -> 213 us  [body(): lax.all_to_all(jnp.stack([hidden] * lax.axis_size(('section', 'shard'))),...]
    all_to_all x0 -> x1, starting transfers between devices: none -> 12 us  [body(): lax.all_to_all(jnp.stack([hidden] * lax.axis_size(('section', 'shard'))),...]
    all_to_all x1, starting transfers between devices: 15.7 us -> 22.5 us  [body(): lax.all_to_all(spread, ('section', 'shard'), split_axis=0, concat_axis=0,...]
    another operation x0 -> x1, local copies, waits for them, and re-layouts: none -> 6.72 us  [body(): jnp.stack([hidden] * lax.axis_size(('section', 'shard')))]
where the time goes in v1:
time: 385 us
  waiting for transfers between devices  222 us (58%)
  blocking collectives  68.5 us (18%)
  starting transfers between devices  34.4 us (9%)
  matrix products  30.8 us (8%)
  local copies, waits for them, and re-layouts  18.4 us (5%)
  other arithmetic  9.4 us (2%)
    all_to_all x1, waiting for transfers between devices, body(): lax.all_to_all(jnp.stack([hidden] * lax.axis_size(('section', 'shard'))),...  213 us
    unnamed x1, blocking collectives  68.5 us
    all_to_all x1, starting transfers between devices, body(): lax.all_to_all(spread, ('section', 'shard'), split_axis=0, concat_axis=0,...  22.5 us
    dot_general x1, matrix products, score_block(): up_out = jnp.dot(normed, up_cols, preferred_element_type=jnp.float32)  14.6 us
    dot_general x1, matrix products, score_block(): gate_out = jnp.dot(normed, gate_cols, preferred_element_type=jnp.float32)  14.6 us
    all_to_all x1, starting transfers between devices, body(): lax.all_to_all(jnp.stack([hidden] * lax.axis_size(('section', 'shard'))),...  12 us
    all_to_all x1, waiting for transfers between devices, body(): lax.all_to_all(spread, ('section', 'shard'), split_axis=0, concat_axis=0,...  8.9 us
  transfers between devices with their start and end apart: 2, of which 2 were waited for; matrix products, arithmetic and copies ran while one was open for 2% of the time, Pallas kernels for 0%

profile of v1, /device:TPU:1, one launch (start us, length us, event | category | flops | bytes accessed | tf_op | source)
XLA Modules:
  0.0 384.8 jit_solution(6730732074478089691)
XLA Ops:
  0.6 0.0 copy-start
  0.6 6.7 %stack.2 = bf16[128,8,8192]{2,1,0:T(8,128)(2,1)} broadcast(bf16[8,8192]{1,0:T(8,128)(2,1)} %param.7), dimensions={1,2} | broadcast | bytes 16908288 | tf_op jit(solution)/shard_map/stack | solution.py:40
  7.4 12.0 %all-to-all-start = ((bf16[128,8,8192]{2,1,0:T(8,128)(2,1)}), bf16[128,8,8192]{2,1,0:T(8,128)(2,1)}, u32[]{:S(2)}, u32[]{:S(2)}) async-start(bf16[128,8,8192]{2,1,0:T(8,128)(2,1)} %stack.2), calls=%async_computation | async-start | bytes 33554432 | tf_op jit(solution)/shard_map/all_to_all | solution.py:39
  19.3 0.7 compare_select_fusion
  20.1 4.3 %scatter_custom_fusion = s32[1024]{0:T(1024)S(1)} fusion(s32[1024]{0:T(1024)S(1)} %bitcast.31, s32[1024]{0:T(1024)S(1)} %iota.3, s32[]{:T(128)} %constant.11.clone.1), kind=kCustom, calls=%fused_computation.34 | custom fusion | bytes 4100 | tf_op jit(solution)/shard_map/scatter | solution.py:27
  24.4 0.6 dynamic-slice
  25.7 0.1 compare_select_fusion.3
  25.8 0.7 gather_fusion.1
  26.5 0.0 copy-start.1
  26.5 213.0 %all-to-all-done = bf16[128,8,8192]{2,1,0:T(8,128)(2,1)} async-done(((bf16[128,8,8192]{2,1,0:T(8,128)(2,1)}), bf16[128,8,8192]{2,1,0:T(8,128)(2,1)}, u32[]{:S(2)}, u32[]{:S(2)}) %all-to-all-start) | async-done | bytes 16777248 | tf_op jit(solution)/shard_map/all_to_all | solution.py:39
  239.4 7.3 %fusion = f32[128,8]{1,0:T(8,128)S(1)} fusion(bf16[128,8,8192]{2,1,0:T(8,128)(2,1)} %all-to-all-done), kind=kLoop, calls=%fused_computation.6 | loop fusion | flops 25164800 | bytes 16781312 | tf_op jit(solution)/shard_map/reduce_sum | solution.py:11
  246.8 0.1 copy.12
  246.9 14.6 %fusion.4 = f32[1024,512]{1,0:T(8,128)S(1)} fusion(bf16[128,8,8192]{2,1,0:T(8,128)(2,1)} %all-to-all-done, f32[8192]{0:T(1024)S(1)} %bitcast.32, f32[128,8]{1,0:T(8,128)S(1)} %copy.12, bf16[1,8192,512]{2,1,0:T(8,128)(2,1)} %param.10), kind=kOutput, calls=%fused_computation.10 | convolution fusion | flops 8623489024 | bytes 27299840 | tf_op jit(solution)/shard_map/dot_general | solution.py:17
  261.6 14.6 %fusion.6 = f32[1024,512]{1,0:T(8,128)S(1)} fusion(bf16[128,8,8192]{2,1,0:T(8,128)(2,1)} %all-to-all-done, f32[8192]{0:T(1024)S(1)} %bitcast.33, f32[128,8]{1,0:T(8,128)S(1)} %copy.12, bf16[1,8192,512]{2,1,0:T(8,128)(2,1)} %param.9), kind=kOutput, calls=%fused_computation.11 | convolution fusion | flops 8623489024 | bytes 27299840 | tf_op jit(solution)/shard_map/dot_general | solution.py:16
  276.2 1.5 fusion.10
  277.7 4.5 %gather_fusion = f32[1024]{0:T(1024)S(1)} fusion(f32[1024]{0:T(1024)S(1)} %bitcast.29, s32[1024]{0:T(1024)S(1)} %fusion.18), kind=kCustom, calls=%fused_computation | custom fusion | bytes 12288 | tf_op jit(solution)/shard_map/gather | solution.py:56
  282.3 68.5 %all-reduce = f32[1024]{0:T(1024)S(1)} all-reduce(f32[1024]{0:T(1024)S(1)} %gather_fusion), channel_id=2, replica_groups=mesh['section'=4,'shard'=32] {'shard'}, use_global_device_ids=true, to_apply=%region_2.3.clone | all-reduce | flops 1024 | bytes 8192
  350.8 0.1 broadcast_select_fusion
  350.8 0.7 scatter_custom_fusion.1
  351.5 0.7 all_to_all.10
  352.2 22.5 %all-to-all-start.1 = ((f32[128,1,8]{2,1,0:T(1,128)}), f32[128,1,8]{2,1,0:T(1,128)S(1)}, u32[]{:S(2)}, u32[]{:S(2)}) async-start(f32[128,1,8]{2,1,0:T(1,128)} %bitcast.10), calls=%async_computation.1 | async-start | bytes 131072 | tf_op jit(solution)/shard_map/all_to_all | solution.py:70
  374.7 0.6 fusion.27
  375.3 8.9 %all-to-all-done.1 = f32[128,1,8]{2,1,0:T(1,128)S(1)} async-done(((f32[128,1,8]{2,1,0:T(1,128)}), f32[128,1,8]{2,1,0:T(1,128)S(1)}, u32[]{:S(2)}, u32[]{:S(2)}) %all-to-all-start.1) | async-done | bytes 4128 | tf_op jit(solution)/shard_map/all_to_all | solution.py:70
  384.2 0.6 bitcast_reduce_fusion
  (12 shorter events, 0.1 us)
Async XLA Ops:
  0.6 25.1 %copy-start = (s32[1024]{0:T(1024)S(1)}, s32[1024]{0:T(1024)}, u32[]{:S(2)}) copy-start(s32[1024]{0:T(1024)} %param.13) | copy-start | bytes 12292
  7.4 17.1 %copy-start.3 = (u32[128]{0:T(128)S(1)}, u32[128]{0:T(128)}, u32[]{:S(2)}) copy-start(u32[128]{0:T(128)} %constant.49) | copy-start | bytes 1540
  7.4 232.1 %all-to-all-start = ((bf16[128,8,8192]{2,1,0:T(8,128)(2,1)}), bf16[128,8,8192]{2,1,0:T(8,128)(2,1)}, u32[]{:S(2)}, u32[]{:S(2)}) async-start(bf16[128,8,8192]{2,1,0:T(8,128)(2,1)} %stack.2), calls=%async_computation | async-start | bytes 33554432 | tf_op jit(solution)/shard_map/all_to_all | solution.py:39
  26.5 220.4 %copy-start.1 = (f32[1,8192]{1,0:T(1,128)S(1)}, f32[1,8192]{1,0:T(1,128)}, u32[]{:S(2)}) copy-start(f32[1,8192]{1,0:T(1,128)} %param.8) | copy-start | bytes 98308
  261.5 14.7 %copy-start.2 = (bf16[1,512]{1,0:T(2,128)(2,1)S(1)}, bf16[1,512]{1,0:T(2,128)(2,1)}, u32[]{:S(2)}) copy-start(bf16[1,512]{1,0:T(2,128)(2,1)} %param.11) | copy-start | bytes 3076
  352.2 32.0 %all-to-all-start.1 = ((f32[128,1,8]{2,1,0:T(1,128)}), f32[128,1,8]{2,1,0:T(1,128)S(1)}, u32[]{:S(2)}, u32[]{:S(2)}) async-start(f32[128,1,8]{2,1,0:T(1,128)} %bitcast.10), calls=%async_computation.1 | async-start | bytes 131072 | tf_op jit(solution)/shard_map/all_to_all | solution.py:70
